TPU v7x, 32 devices: a whole 2x2x4 slice. The times are simulated.
32 devices in a mesh: dp: 4 (over x, core), expert: 8 (over z, y).
Axes of the slice: x: 2, y: 2, z: 4, core: 2. Of those that a mesh axis runs over, the one named last changes fastest.
Arguments:
- embeds: bfloat16 [8192, 1152], P(('dp', 'expert')), may hold values from -6 to 6
- trunk_gain: float32 [1152], replicated, may hold values from 0.5 to 1.5
- trunk_weight: bfloat16 [1152, 1152], replicated, may hold values from -0.1875 to 0.1875
- w_gate: bfloat16 [32, 1152, 1024], P(('dp', 'expert')), may hold values from -0.1875 to 0.1875
- w_up: bfloat16 [32, 1152, 1024], P(('dp', 'expert')), may hold values from -0.1875 to 0.1875
- w_down: bfloat16 [32, 1024, 1152], P(('dp', 'expert')), may hold values from -0.1875 to 0.1875
- tags: int32 [8192], P(('dp', 'expert')), may hold values from 0 to 31, as said below
- plan: int32 [32], replicated, may hold values from 0 to 31, as said below
- helper: int32 [8192], P(('dp', 'expert')), may hold values from 0 to 31, as said below
- cotangent: bfloat16 [8192, 1152], P(('dp', 'expert')), may hold values from -0.59765625 to 0.59765625
Outputs:
- grad_gate: bfloat16 [32, 1152, 1024], P(('dp', 'expert'))
- grad_up: bfloat16 [32, 1152, 1024], P(('dp', 'expert'))
- grad_down: bfloat16 [32, 1024, 1152], P(('dp', 'expert'))
- grad_trunk: float32 [1152, 1152], P(('dp', 'expert'))
Inputs may be any that keep to these rules, and one draw needn't show every extreme that they name: Each token's helper equals its tag, except for tokens tagged with the expert plan[0], which may go to any device. Each device sends exactly 8 tokens to every device (numbered in the order dp then expert). Every device other than device plan[0] receives exactly 8 tokens tagged plan[0]; device plan[0] receives only tokens tagged plan[0]. `tags`: see helper. A permutation of the 32 experts; only plan[0] is served by helpers.
All inputs are finite; a program needn't handle non-finite values.
Results may differ from a plain program's by a relative error of at most 0.003.
The roundings to bfloat16 on the way count: a program that leaves them out, or rounds other values in their place, can miss the bound.
Values may be sent and summed in bfloat16 or wider, within the bound.
A program may use at most 128 MiB of HBM per device.

v0:
```python
import functools

import jax
import jax.numpy as jnp
from jax import lax
from jax.experimental import pallas as pl
from jax.experimental.pallas import tpu as pltpu
from jax.sharding import PartitionSpec as P

LANES = 128
TILE = 16
MESH = pl.DeviceIdType.MESH


def padded(value, multiple):
    return -(-value // multiple) * multiple


def flat_index(experts_axis):
    return lax.axis_index("dp") * experts_axis + lax.axis_index("expert")


def place(flat, experts_axis):
    return (flat // experts_axis, flat % experts_axis)


def flipped(me, bit):
    weight = 1 << bit
    return me + (1 - 2 * ((me // weight) % 2)) * weight


def greet_all(n, experts_axis):
    me = flat_index(experts_axis)
    barrier = pltpu.get_barrier_semaphore()

    def greet(step, carry):
        pl.semaphore_signal(
            barrier,
            inc=1,
            device_id=place(lax.rem(me + step, n), experts_axis),
            device_id_type=MESH,
        )
        return carry

    lax.fori_loop(1, n, greet, 0)
    pl.semaphore_wait(barrier, n - 1)


def greet_bits(bits, experts_axis):
    me = flat_index(experts_axis)
    barrier = pltpu.get_barrier_semaphore()
    for bit in range(bits):
        pl.semaphore_signal(
            barrier, inc=1, device_id=place(flipped(me, bit), experts_axis), device_id_type=MESH
        )
    pl.semaphore_wait(barrier, bits)


def exchange_kernel(n, experts_axis, send_ref, out_ref, send_sem, recv_sem, own_sem):
    me = flat_index(experts_axis)
    greet_all(n, experts_axis)
    own = pltpu.make_async_copy(send_ref.at[me], out_ref.at[me], own_sem)
    own.start()

    def copy_to(step):
        to = lax.rem(me + step, n)
        return pltpu.make_async_remote_copy(
            src_ref=send_ref.at[to],
            dst_ref=out_ref.at[me],
            send_sem=send_sem.at[to],
            recv_sem=recv_sem.at[me],
            device_id=place(to, experts_axis),
            device_id_type=MESH,
        )

    def copy_from(step):
        source = lax.rem(me + step, n)
        return pltpu.make_async_remote_copy(
            src_ref=send_ref.at[source],
            dst_ref=out_ref.at[source],
            send_sem=send_sem.at[source],
            recv_sem=recv_sem.at[source],
            device_id=place(source, experts_axis),
            device_id_type=MESH,
        )

    def start(step, carry):
        copy_to(step).start()
        return carry

    def finish(step, carry):
        copy = copy_from(step)
        copy.wait_send()
        copy.wait_recv()
        return carry

    lax.fori_loop(1, n, start, 0)
    own.wait()
    lax.fori_loop(1, n, finish, 0)


def exchange(send, n, experts_axis):
    return pl.pallas_call(
        functools.partial(exchange_kernel, n, experts_axis),
        out_shape=jax.ShapeDtypeStruct(send.shape, send.dtype),
        in_specs=[pl.BlockSpec(memory_space=pltpu.VMEM)],
        out_specs=pl.BlockSpec(memory_space=pltpu.VMEM),
        scratch_shapes=[
            pltpu.SemaphoreType.DMA((n,)),
            pltpu.SemaphoreType.DMA((n,)),
            pltpu.SemaphoreType.DMA,
        ],
        compiler_params=pltpu.CompilerParams(
            collective_id=0, has_side_effects=True, vmem_limit_bytes=40 * 1024 * 1024
        ),
    )(send)


def axis_orders(n, experts_axis):
    bits = n.bit_length() - 1
    core = experts_axis.bit_length() - 1
    others = [b for b in range(bits) if b != core]
    low = others[0]
    high = others[-1]
    middle = others[1:-1]
    return core, [
        [high, low] + middle,
        [low] + middle + [high],
        middle + [high, low],
    ]


def column_groups(width):
    tiles = width // LANES
    cuts = [(tiles * g) // 3 * LANES for g in range(4)]
    return [(cuts[g], cuts[g + 1] - cuts[g]) for g in range(3)]


def gather_kernel(n, experts_axis, width, mine_ref, out_ref, *scratch):
    bits = n.bit_length() - 1
    me = flat_index(experts_axis)
    core, orders = axis_orders(n, experts_axis)
    held, send_sem, recv_sem = scratch[:3], scratch[3], scratch[4]
    for group, (first, wide) in enumerate(column_groups(width)):
        held[group][0] = mine_ref[:, first : first + wide]
    greet_bits(bits, experts_axis)
    plans = [order[::-1] + [core] for order in orders]
    for stage in range(bits):
        count = 1 << stage
        copies = []
        for group in range(3):
            bit = plans[group][stage]
            copy = pltpu.make_async_remote_copy(
                src_ref=held[group].at[pl.ds(0, count)],
                dst_ref=held[group].at[pl.ds(count, count)],
                send_sem=send_sem.at[stage, group],
                recv_sem=recv_sem.at[stage, group],
                device_id=place(flipped(me, bit), experts_axis),
                device_id_type=MESH,
            )
            copy.start()
            copies.append(copy)
        for copy in copies:
            copy.wait()
    for group, (first, wide) in enumerate(column_groups(width)):
        for slot in range(n):
            offset = sum(
                1 << plans[group][stage] for stage in range(bits) if (slot >> stage) & 1
            )
            out_ref[offset, :, first : first + wide] = held[group][slot]


def gather(mine, n, experts_axis):
    rows, width = mine.shape
    bits = n.bit_length() - 1
    return pl.pallas_call(
        functools.partial(gather_kernel, n, experts_axis, width),
        out_shape=jax.ShapeDtypeStruct((n, rows, width), mine.dtype),
        in_specs=[pl.BlockSpec(memory_space=pltpu.VMEM)],
        out_specs=pl.BlockSpec(memory_space=pltpu.VMEM),
        scratch_shapes=[
            pltpu.VMEM((n, rows, wide), mine.dtype) for _, wide in column_groups(width)
        ]
        + [pltpu.SemaphoreType.DMA((bits, 3)), pltpu.SemaphoreType.DMA((bits, 3))],
        compiler_params=pltpu.CompilerParams(
            collective_id=1, has_side_effects=True, vmem_limit_bytes=48 * 1024 * 1024
        ),
    )(mine)


def stage_types(bits):
    return [jnp.bfloat16 if stage < 3 else jnp.float32 for stage in range(bits)]


def reduce_kernel(n, experts_axis, block, width, left_ref, right_ref, out_ref, *scratch):
    bits = n.bit_length() - 1
    me = flat_index(experts_axis)
    core, orders = axis_orders(n, experts_axis)
    plans = [[core] + order for order in orders]
    groups = column_groups(width)
    types = stage_types(bits)
    kept = [[scratch[3 * (s * 3 + g)] for g in range(3)] for s in range(bits)]
    sent = [[scratch[3 * (s * 3 + g) + 1] for g in range(3)] for s in range(bits)]
    came = [[scratch[3 * (s * 3 + g) + 2] for g in range(3)] for s in range(bits)]
    send_sem, recv_sem = scratch[9 * bits], scratch[9 * bits + 1]
    greet_bits(bits, experts_axis)

    def transfer(stage, group):
        return pltpu.make_async_remote_copy(
            src_ref=sent[stage][group],
            dst_ref=came[stage][group],
            send_sem=send_sem.at[stage, group],
            recv_sem=recv_sem.at[stage, group],
            device_id=place(flipped(me, plans[group][stage]), experts_axis),
            device_id_type=MESH,
        )

    def side_of(bit):
        return (me // (1 << bit)) % 2

    chunk = experts_axis * block
    spans = n // (2 * experts_axis)

    def first_half(group, side, into, kind):
        first, wide = groups[group]
        for span in range(spans):
            at = pl.multiple_of((2 * span + side) * chunk, chunk)
            product = jnp.dot(
                left_ref[pl.ds(at, chunk), :],
                right_ref[:, first : first + wide],
                preferred_element_type=jnp.float32,
            )
            for item in range(experts_axis):
                into[span * experts_axis + item] = product[
                    item * block : (item + 1) * block
                ].astype(kind)

    for group in range(3):
        first_half(group, 1 - side_of(core), sent[0][group], types[0])
        transfer(0, group).start()
    for group in range(3):
        first_half(group, side_of(core), kept[0][group], jnp.float32)

    left = [[b for b in range(bits - 1, -1, -1) if b != core] for _ in groups]
    for stage in range(1, bits):
        half = n >> (stage + 1)
        for group in range(3):
            bit = plans[group][stage]
            low = 1 << (len(left[group]) - left[group].index(bit) - 1)
            left[group].remove(bit)
            mine = side_of(bit)

            def move(side, into, kind, low=low, stage=stage, group=group, half=half):
                def one(item, carry):
                    at = (item // low) * (2 * low) + side * low + item % low
                    into[item] = (
                        kept[stage - 1][group][at]
                        + came[stage - 1][group][at].astype(jnp.float32)
                    ).astype(kind)
                    return carry

                lax.fori_loop(0, half, one, 0)

            transfer(stage - 1, group).wait()
            move(1 - mine, sent[stage][group], types[stage])
            transfer(stage, group).start()
            move(mine, kept[stage][group], jnp.float32)
    for group, (first, wide) in enumerate(groups):
        transfer(bits - 1, group).wait()
        out_ref[:, first : first + wide] = kept[bits - 1][group][0] + came[bits - 1][group][
            0
        ].astype(jnp.float32)


def reduce_scatter(left, right, block, n, experts_axis):
    width = right.shape[1]
    bits = n.bit_length() - 1
    types = stage_types(bits)
    scratch = []
    for stage in range(bits):
        half = n >> (stage + 1)
        for _, wide in column_groups(width):
            scratch.append(pltpu.VMEM((half, block, wide), jnp.float32))
            scratch.append(pltpu.VMEM((half, block, wide), types[stage]))
            scratch.append(pltpu.VMEM((half, block, wide), types[stage]))
    return pl.pallas_call(
        functools.partial(reduce_kernel, n, experts_axis, block, width),
        out_shape=jax.ShapeDtypeStruct((block, width), jnp.float32),
        in_specs=[pl.BlockSpec(memory_space=pltpu.VMEM)] * 2,
        out_specs=pl.BlockSpec(memory_space=pltpu.VMEM),
        scratch_shapes=scratch
        + [pltpu.SemaphoreType.DMA((bits, 3)), pltpu.SemaphoreType.DMA((bits, 3))],
        compiler_params=pltpu.CompilerParams(
            collective_id=2, has_side_effects=True, vmem_limit_bytes=52 * 1024 * 1024
        ),
    )(left, right)


def lines_of(blocks, count, rows, first):
    lines = blocks.shape[0]
    wanted = jnp.arange(lines // rows * count, dtype=jnp.int32)
    wanted = wanted // count * rows + first + wanted % count
    chosen = wanted[:, None] == jnp.arange(lines, dtype=jnp.int32)[None, :]
    return jnp.dot(
        chosen.astype(jnp.bfloat16), blocks, preferred_element_type=jnp.float32
    ).astype(jnp.bfloat16)


def trunk(rows, gain, weight):
    values = rows.astype(jnp.float32)
    factor = lax.rsqrt(jnp.mean(values * values, axis=1, keepdims=True) + 1e-06)
    normed = (values * factor * gain).astype(jnp.bfloat16)
    hidden = values + jnp.dot(normed, weight, preferred_element_type=jnp.float32)
    return normed, hidden.astype(jnp.bfloat16)


def dot_t(a, b):
    return lax.dot_general(a, b, (((1,), (1,)), ((), ())), preferred_element_type=jnp.float32)


def t_dot(a, b):
    return lax.dot_general(a, b, (((0,), (0,)), ((), ())), preferred_element_type=jnp.float32)


def through_expert(hidden, cotan, gate_w, up_w, down_w):
    gate_pre = jnp.dot(hidden, gate_w, preferred_element_type=jnp.float32)
    up_pre = jnp.dot(hidden, up_w, preferred_element_type=jnp.float32)
    sigma = jax.nn.sigmoid(gate_pre)
    silu_val = gate_pre * sigma
    active = (silu_val * up_pre).astype(jnp.bfloat16)
    d_active = dot_t(cotan, down_w)
    d_gate = (d_active * up_pre * sigma * (1.0 + gate_pre * (1.0 - sigma))).astype(jnp.bfloat16)
    d_up = (d_active * silu_val).astype(jnp.bfloat16)
    d_rows = (dot_t(d_gate, gate_w) + dot_t(d_up, up_w)).astype(jnp.bfloat16)
    return active, d_gate, d_up, d_rows


def body(embeds, trunk_gain, trunk_weight, w_gate, w_up, w_down, tags, plan, helper, cotangent):
    n = lax.axis_size(("dp", "expert"))
    experts_axis = lax.axis_size("expert")
    device = flat_index(experts_axis)
    hot_expert = plan[0]
    tokens, feature = embeds.shape
    capacity = tokens // n
    hot_slots = tokens // 32
    rows = padded(2 * capacity, TILE)
    gate_w, up_w, down_w = w_gate[0], w_up[0], w_down[0]

    token = jnp.arange(tokens, dtype=jnp.int32)
    before = (helper[:, None] == helper[None, :]) & (token[:, None] > token[None, :])
    slot = jnp.sum(before.astype(jnp.int32), axis=1)
    target = helper * rows + slot
    line = jnp.arange(n * rows, dtype=jnp.int32)
    pick = jnp.concatenate(
        [line[:, None] == target[None, :], line[:, None] == target[None, :] + capacity], axis=1
    ).astype(jnp.bfloat16)
    flagged = ((tags == hot_expert) & (helper != hot_expert)).astype(jnp.bfloat16)
    flag_lanes = jnp.broadcast_to(flagged[:, None], (tokens, LANES))
    content = jnp.concatenate(
        [
            jnp.concatenate([embeds, flag_lanes], axis=1),
            jnp.concatenate([cotangent, jnp.zeros_like(flag_lanes)], axis=1),
        ],
        axis=0,
    )
    send = jnp.dot(pick, content, preferred_element_type=jnp.float32).astype(jnp.bfloat16)
    got = exchange(send.reshape(n, rows, feature + LANES), n, experts_axis)
    got = got.reshape(n * rows, feature + LANES)
    got_wide = lines_of(got, capacity, rows, 0)
    got_embeds = got_wide[:, :feature]
    got_cotan = lines_of(got[:, :feature], capacity, rows, capacity)
    flags = got_wide[:, feature] > 0

    rank = jnp.sum((flags[None, :] & (token[:, None] > token[None, :])).astype(jnp.int32), axis=1)
    picker = (rank[None, :] == jnp.arange(hot_slots, dtype=jnp.int32)[:, None]) & flags[None, :]
    picker = picker.astype(jnp.bfloat16)
    hot = jnp.concatenate(
        [
            jnp.dot(picker, got_embeds, preferred_element_type=jnp.float32),
            jnp.dot(picker, got_cotan, preferred_element_type=jnp.float32),
        ],
        axis=0,
    ).astype(jnp.bfloat16)
    pooled = gather(hot, n, experts_axis)
    pooled = pooled.reshape(n * 2 * hot_slots, feature)
    hot_embeds = lines_of(pooled, hot_slots, 2 * hot_slots, 0)
    hot_cotan = lines_of(pooled, hot_slots, 2 * hot_slots, hot_slots)
    is_owner = device == hot_expert
    hot_cotan = jnp.where(is_owner, hot_cotan, jnp.zeros_like(hot_cotan))
    own_cotan = jnp.where(flags[:, None], jnp.zeros_like(got_cotan), got_cotan)

    all_embeds = jnp.concatenate([got_embeds, hot_embeds], axis=0)
    all_cotan = jnp.concatenate([own_cotan, hot_cotan], axis=0)
    normed, hidden = trunk(all_embeds, trunk_gain, trunk_weight)
    active, d_gate, d_up, d_rows = through_expert(hidden, all_cotan, gate_w, up_w, down_w)

    share = feature // n
    block = padded(share, TILE // 2)
    column = jnp.arange(n * block, dtype=jnp.int32)
    source = jnp.where(column % block < share, column // block * share + column % block, -1)
    spread = (source[:, None] == jnp.arange(feature, dtype=jnp.int32)[None, :]).astype(
        jnp.bfloat16
    )
    normed_lines = dot_t(spread, normed).astype(jnp.bfloat16)
    grad_trunk = reduce_scatter(normed_lines, d_rows, block, n, experts_axis)[:share]

    grad_gate = t_dot(hidden, d_gate).astype(jnp.bfloat16)[None]
    grad_up = t_dot(hidden, d_up).astype(jnp.bfloat16)[None]
    grad_down = t_dot(active, all_cotan).astype(jnp.bfloat16)[None]
    return (grad_gate, grad_up, grad_down, grad_trunk)


def solution(mesh):
    spread_rows = P(("dp", "expert"), None)
    spread_first = P(("dp", "expert"), None, None)
    return jax.shard_map(
        body,
        mesh=mesh,
        in_specs=(
            spread_rows,
            P(),
            P(),
            spread_first,
            spread_first,
            spread_first,
            P(("dp", "expert")),
            P(),
            P(("dp", "expert")),
            spread_rows,
        ),
        out_specs=(spread_first, spread_first, spread_first, spread_rows),
        check_vma=False,
    )
```

profile of v0, /device:TPU:0, one launch (start us, length us, event | category | flops | bytes accessed | tf_op | source)
XLA Modules:
  0.0 121.6 jit_solution(13947391710105746773)
XLA Ops:
  1.4 1.3 %and_convert_fusion = bf16[256]{0:T(256)(128)(2,1)S(1)} fusion(s32[256]{0:T(256)} %param.18, s32[256]{0:T(256)} %param.16, s32[]{:T(128)} %bitcast.47), kind=kLoop, calls=%fused_computation.101 | loop fusion | flops 1024 | bytes 2564 | tf_op jit(solution)/shard_map/convert_element_type | solution.py:357
  2.8 0.9 convert_reduce_fusion.1
  3.7 0.7 broadcast_add_fusion
  4.7 2.1 %convolution_convert_fusion.3 = bf16[512,1280]{1,0:T(8,128)(2,1)S(1)} fusion(bf16[256,1152]{1,0:T(8,128)(2,1)} %param.19, bf16[256,128]{1,0:T(8,128)(2,1)S(1)} %broadcast_in_dim.14, bf16[256,1152]{1,0:T(8,128)(2,1)} %param.10, pred[512,256]{1,0:T(32,128)(4,1)S(1)} %get-tuple-element.10, pred[512,256]{1,0:T(32,128)(4,1)S(1)} %get-tuple-element.11), kind=kOutput, calls=%fused_computation.14 | convolution fusion | flops 677249024 | bytes 2818048 | tf_op jit(solution)/shard_map/dot_general | solution.py:366
  6.8 35.5 %shard_map.129 = bf16[32,16,1280]{2,1,0:T(8,128)(2,1)S(1)} custom-call(bf16[32,16,1280]{2,1,0:T(8,128)(2,1)S(1)} %bitcast.44), custom_call_target="tpu_custom_call" | custom-call | tf_op jit(solution)/shard_map/pallas_call | solution.py:103
  42.3 0.5 convolution_convert_fusion.7
  43.0 0.6 broadcast_select_fusion
  43.8 0.2 convolution_convert_fusion.9
  44.1 20.8 %shard_map.130 = bf16[32,16,1152]{2,1,0:T(8,128)(2,1)S(1)} custom-call(bf16[16,1152]{1,0:T(8,128)(2,1)S(1)} %pad_maximum_fusion.6.mine_ref), custom_call_target="tpu_custom_call" | custom-call | tf_op jit(solution)/shard_map/pallas_call | solution.py:176
  64.9 0.6 fusion.9
  65.5 0.6 convolution_convert_fusion.5
  66.1 0.3 fusion.10
  66.4 1.9 %fusion.4 = bf16[512,1152]{1,0:T(8,128)(2,1)S(1)} fusion(bf16[1152,1152]{1,0:T(8,128)(2,1)S(1)} %copy-done, f32[1152]{0:T(1024)S(1)} %copy-done.4, f32[512]{0:T(512)S(1)} %add_rsqrt_fusion, bf16[256,1152]{1,0:T(8,128)(2,1)S(1)} %convolution_convert_fusion.5, bf16[256,1152]{1,0:T(8,128)(2,1)S(1)} %slice.20), kind=kOutput, calls=%fused_computation.12 | convolution fusion | flops 1366622208 | bytes 5020160 | tf_op jit(solution)/shard_map/dot_general | solution.py:313
  68.3 3.1 %fusion.6.left_ref = bf16[1280,512]{1,0:T(8,128)(2,1)} fusion(s32[1280]{0:T(1024)S(1)} %fusion.56, f32[1152]{0:T(1024)S(1)} %copy-done.4, f32[512]{0:T(512)S(1)} %add_rsqrt_fusion, bf16[256,1152]{1,0:T(8,128)(2,1)S(1)} %convolution_convert_fusion.5, bf16[256,1152]{1,0:T(8,128)(2,1)S(1)} %slice.20), kind=kOutput, calls=%fused_computation.15 | convolution fusion | flops 1516208128 | bytes 2502144 | tf_op jit(solution)/shard_map/dot_general | solution.py:318
  71.4 1.6 %fusion.15 = f32[512,1024]{1,0:T(8,128)S(1)} fusion(bf16[512,1152]{1,0:T(8,128)(2,1)S(1)} %fusion.4, bf16[1,1152,1024]{2,1,0:T(8,128)(2,1)S(1)} %copy-done.2), kind=kOutput, calls=%fused_computation.29 | convolution fusion | flops 1207959552 | bytes 5636096 | tf_op jit(solution)/shard_map/dot_general | solution.py:326
  73.1 1.5 %fusion.18 = f32[512,1024]{1,0:T(8,128)S(1)} fusion(bf16[512,1152]{1,0:T(8,128)(2,1)S(1)} %fusion.4, bf16[1,1152,1024]{2,1,0:T(8,128)(2,1)S(1)} %copy-done.3), kind=kOutput, calls=%fused_computation.32 | convolution fusion | flops 1207959552 | bytes 5636096 | tf_op jit(solution)/shard_map/dot_general | solution.py:327
  74.8 2.1 %multiply_convert_fusion.1 = (bf16[512,1024]{1,0:T(8,128)(2,1)S(1)}, bf16[512,1024]{1,0:T(8,128)(2,1)S(1)}) fusion(f32[512,1024]{1,0:T(8,128)S(1)} %fusion.15, f32[512,1024]{1,0:T(8,128)S(1)} %fusion.18, bf16[1,1024,1152]{2,1,0:T(8,128)(2,1)S(1)} %copy-done.1, bf16[256,1152]{1,0:T(8,128)(2,1)S(1)} %fusion.9, bf16[256,1152]{1,0:T(8,128)(2,1)S(1)} %get-tuple-element.8), kind=kOutput, calls=%fused_computation.39 | convolution fusion | flops 1217134592 | bytes 9830400 | tf_op jit(solution)/shard_map/dot_general | solution.py:318
  76.8 3.1 %fusion.3 = bf16[1,1024,1152]{2,1,0:T(8,128)(2,1)} fusion(f32[512,1024]{1,0:T(8,128)S(1)} %fusion.18, bf16[256,1152]{1,0:T(8,128)(2,1)S(1)} %fusion.9, bf16[256,1152]{1,0:T(8,128)(2,1)S(1)} %get-tuple-element.8, f32[512,1024]{1,0:T(8,128)S(1)} %fusion.15), kind=kOutput, calls=%fused_computation.11 | convolution fusion | flops 1214644224 | bytes 7733248 | tf_op jit(solution)/shard_map/dot_general | solution.py:322
  79.9 3.0 %fusion.2 = bf16[1,1152,1024]{2,1,0:T(8,128)(2,1)} fusion(bf16[512,1152]{1,0:T(8,128)(2,1)S(1)} %fusion.4, bf16[512,1024]{1,0:T(8,128)(2,1)S(1)} %get-tuple-element.6), kind=kOutput, calls=%fused_computation.10 | convolution fusion | flops 1209139200 | bytes 4587520 | tf_op jit(solution)/shard_map/dot_general | solution.py:322
  82.9 2.8 %fusion.1 = bf16[1,1152,1024]{2,1,0:T(8,128)(2,1)} fusion(bf16[512,1152]{1,0:T(8,128)(2,1)S(1)} %fusion.4, bf16[512,1024]{1,0:T(8,128)(2,1)S(1)} %get-tuple-element.7), kind=kOutput, calls=%fused_computation.9 | convolution fusion | flops 1209139200 | bytes 4587520 | tf_op jit(solution)/shard_map/dot_general | solution.py:322
  85.7 1.6 %fusion.13 = f32[512,1152]{1,0:T(8,128)S(1)} fusion(bf16[512,1024]{1,0:T(8,128)(2,1)S(1)} %get-tuple-element.7, bf16[1,1152,1024]{2,1,0:T(8,128)(2,1)S(1)} %copy-done.2), kind=kOutput, calls=%fused_computation.27 | convolution fusion | flops 1207959552 | bytes 5767168 | tf_op jit(solution)/shard_map/dot_general | solution.py:318
  87.3 1.6 %fusion.5.right_ref = bf16[512,1152]{1,0:T(8,128)(2,1)S(1)} fusion(f32[512,1152]{1,0:T(8,128)S(1)} %fusion.13, bf16[512,1024]{1,0:T(8,128)(2,1)S(1)} %get-tuple-element.6, bf16[1,1152,1024]{2,1,0:T(8,128)(2,1)S(1)} %copy-done.3), kind=kOutput, calls=%fused_computation.13 | convolution fusion | flops 1209139200 | bytes 6946816 | tf_op jit(solution)/shard_map/dot_general | solution.py:318
  88.9 32.0 %shard_map.131 = f32[40,1152]{1,0:T(8,128)S(1)} custom-call(bf16[1280,512]{1,0:T(8,128)(2,1)} %fusion.6.left_ref, bf16[512,1152]{1,0:T(8,128)(2,1)S(1)} %fusion.5.right_ref), custom_call_target="tpu_custom_call" | custom-call | tf_op jit(solution)/shard_map/pallas_call | solution.py:286
  120.9 0.7 copy.19
  (21 shorter events, 1.0 us)
Async XLA Ops:
  0.6 65.7 %copy-start = (bf16[1152,1152]{1,0:T(8,128)(2,1)S(1)}, bf16[1152,1152]{1,0:T(8,128)(2,1)}, u32[]{:S(2)}) copy-start(bf16[1152,1152]{1,0:T(8,128)(2,1)} %param.12) | copy-start | bytes 7962628
  64.9 1.5 %copy-start.4 = (f32[1152]{0:T(1024)S(1)}, f32[1152]{0:T(1024)}, u32[]{:S(2)}) copy-start(f32[1152]{0:T(1024)} %param.11) | copy-start | bytes 13828
  68.3 3.1 %copy-start.2 = (bf16[1,1152,1024]{2,1,0:T(8,128)(2,1)S(1)}, bf16[1,1152,1024]{2,1,0:T(8,128)(2,1)}, u32[]{:S(2)}) copy-start(bf16[1,1152,1024]{2,1,0:T(8,128)(2,1)} %param.13) | copy-start | bytes 7077892
  71.4 1.7 %copy-start.3 = (bf16[1,1152,1024]{2,1,0:T(8,128)(2,1)S(1)}, bf16[1,1152,1024]{2,1,0:T(8,128)(2,1)}, u32[]{:S(2)}) copy-start(bf16[1,1152,1024]{2,1,0:T(8,128)(2,1)} %param.14) | copy-start | bytes 7077892
  73.1 1.7 %copy-start.1 = (bf16[1,1024,1152]{2,1,0:T(8,128)(2,1)S(1)}, bf16[1,1024,1152]{2,1,0:T(8,128)(2,1)}, u32[]{:S(2)}) copy-start(bf16[1,1024,1152]{2,1,0:T(8,128)(2,1)} %param.15) | copy-start | bytes 7077892
where the time goes:
time: 122 us
  Pallas kernels  88.3 us (72%)
  matrix products  26.9 us (22%)
  other arithmetic  3.69 us (3%)
  between operations  1.62 us (1%)
    pallas_call x1, Pallas kernels, exchange(): pl.pallas_call(functools.partial(exchange_kernel, n, experts_axis), out_s...  35.5 us
    pallas_call x1, Pallas kernels, reduce_scatter(): pl.pallas_call(functools.partial(reduce_kernel, n, experts_axis, block, w...  32 us
    pallas_call x1, Pallas kernels, gather(): pl.pallas_call(functools.partial(gather_kernel, n, experts_axis, width),...  20.8 us
    dot_general x3, matrix products, t_dot(): lax.dot_general(a, b, (((0,), (0,)), ((), ())), preferred_element_type=jn...  8.91 us
    dot_general x4, matrix products, dot_t(): lax.dot_general(a, b, (((1,), (1,)), ((), ())), preferred_element_type=jn...  8.3 us

commit v1 on v0

--- a/solution.py
+++ b/solution.py
@@ -1,4 +1,5 @@
 import functools
+import types
 
 import jax
 import jax.numpy as jnp
@@ -10,6 +11,8 @@
 LANES = 128
 TILE = 16
 MESH = pl.DeviceIdType.MESH
+MARK, EMB, COT = range(3)
+VMEM_BYTES = 45 * 1024 * 1024
 
 
 def padded(value, multiple):
@@ -410,11 +413,535 @@
     return (grad_gate, grad_up, grad_down, grad_trunk)
 
 
+def bit_of(me, bit):
+    return (me // (1 << bit)) % 2
+
+
+def iota(shape, dim):
+    return lax.broadcasted_iota(jnp.int32, shape, dim)
+
+
+def as_ones(mask, kind=jnp.bfloat16):
+    return jnp.where(mask, 1.0, 0.0).astype(kind)
+
+
+def reduce_orders(n, experts_axis):
+    bits = n.bit_length() - 1
+    core = experts_axis.bit_length() - 1
+    others = [b for b in range(bits) if b != core]
+    low, high, middle = others[0], others[-1], others[1:-1]
+    return [core, high, low] + middle, [core, low, high] + middle
+
+
+def reduce_widths(width):
+    widths = [2 * LANES] * (width // (2 * LANES))
+    if width % (2 * LANES):
+        widths.append(width % (2 * LANES))
+    starts = [sum(widths[:g]) for g in range(len(widths))]
+    return list(zip(starts, widths))
+
+
+def fused_kernel(n, experts_axis, hot_slots, names, *refs):
+    plain, tree = names
+    r = types.SimpleNamespace(
+        **dict(zip(plain, refs)), **jax.tree.unflatten(tree, refs[len(plain) :])
+    )
+    bits = n.bit_length() - 1
+    tokens, feature = r.emb.shape
+    hidden_units = r.wg.shape[1]
+    capacity = tokens // n
+    hot_rows = n * hot_slots
+    share = feature // n
+    me = flat_index(experts_axis)
+    wide_groups = column_groups(feature)
+    core, gather_orders = axis_orders(n, experts_axis)
+    gather_plans = [order[::-1] + [core] for order in gather_orders]
+    reduce_groups = reduce_widths(feature)
+    orders = reduce_orders(n, experts_axis)
+    layout = orders[0]
+
+    barrier = pltpu.get_barrier_semaphore()
+
+    def greet(step, carry):
+        pl.semaphore_signal(
+            barrier,
+            inc=1,
+            device_id=place(lax.rem(me + step, n), experts_axis),
+            device_id_type=MESH,
+        )
+        return carry
+
+    pairs = (
+        (r.tags_hbm, r.tags),
+        (r.plan_hbm, r.plan),
+        (r.helper_hbm, r.helper),
+        (r.emb_hbm, r.emb),
+        (r.cot_hbm, r.cot),
+        (r.gain_hbm, r.gain),
+        (r.tw_hbm, r.tw),
+        (r.wg_hbm.at[0], r.wg),
+        (r.wu_hbm.at[0], r.wu),
+        (r.wd_hbm.at[0], r.wd),
+    )
+    loads = [
+        pltpu.make_async_copy(far, near, r.load_sem.at[index])
+        for index, (far, near) in enumerate(pairs)
+    ]
+    for load in loads[:4]:
+        load.start()
+    lax.fori_loop(1, n, greet, 0)
+    for load in loads[4:]:
+        load.start()
+    for load in loads[:3]:
+        load.wait()
+
+    helper = r.helper[...]
+    popular = r.plan[0:1, 0:1]
+    foreign = (r.tags[...] == popular) & (helper != popular)
+    to_device = iota((n, tokens), 0) == helper
+    ahead = as_ones(iota((tokens, tokens), 0) < iota((tokens, tokens), 1))
+    to_ones = as_ones(to_device)
+    count = jnp.dot(to_ones, ahead, preferred_element_type=jnp.float32)
+    slot = jnp.sum(jnp.where(to_device, count, 0.0), axis=0, keepdims=True).astype(jnp.int32)
+    target = helper * capacity + slot
+    pick = as_ones(iota((tokens, tokens), 0) == target)
+    marked = as_ones((iota((LANES, tokens), 0) == slot) & foreign)
+    marks = dot_t(to_ones, marked)
+    for device in range(n):
+        r.out[MARK][device] = marks[device : device + 1]
+
+    def packed(whole):
+        rows = jnp.dot(pick, whole[...], preferred_element_type=jnp.float32)
+        return rows.reshape(n, capacity, feature).astype(jnp.bfloat16)
+
+    loads[3].wait()
+    r.out[EMB][...] = packed(r.emb)
+
+    def exchange_copy(kind, step, arriving):
+        other = lax.rem(me + step, n)
+        return pltpu.make_async_remote_copy(
+            src_ref=r.out[kind].at[other],
+            dst_ref=r.into[kind].at[other if arriving else me],
+            send_sem=r.send_sem.at[kind, other],
+            recv_sem=r.recv_sem.at[kind, other if arriving else me],
+            device_id=place(other, experts_axis),
+            device_id_type=MESH,
+        )
+
+    def start_kinds(first, last, *some):
+        def start(step, carry):
+            for kind in some:
+                exchange_copy(kind, step, False).start()
+            return carry
+
+        lax.fori_loop(first, last, start, 0)
+
+    def start_batch(batch):
+        cuts = [1 + (n - 1) * at // (bits + 1) for at in range(bits + 2)]
+        start_kinds(cuts[batch], cuts[batch + 1], COT)
+
+    def finish_kind(kind):
+        def finish(step, carry):
+            copy = exchange_copy(kind, step, True)
+            copy.wait_send()
+            copy.wait_recv()
+            return carry
+
+        lax.fori_loop(1, n, finish, 0)
+
+    own = [
+        pltpu.make_async_copy(r.out[kind].at[me], r.into[kind].at[me], r.own_sem.at[kind])
+        for kind in (MARK, EMB, COT)
+    ]
+
+    pl.semaphore_wait(barrier, n - 1)
+    start_kinds(1, n, MARK, EMB)
+    own[MARK].start()
+    own[EMB].start()
+    loads[4].wait()
+    r.out[COT][...] = packed(r.cot)
+    start_batch(0)
+    own[COT].start()
+
+    place_row = iota((feature, 1), 0)
+    block = jnp.floor((place_row.astype(jnp.float32) + 0.5) / share).astype(jnp.int32)
+    source = place_row - block * share
+    for position, bit in enumerate(layout):
+        part = jnp.right_shift(block, bits - 1 - position) & 1
+        source = source + part * (share << bit)
+    r.order[...] = as_ones(source == iota((feature, feature), 1))
+
+    def gather_copy(kind, stage, group):
+        held = r.held[kind - EMB][group]
+        size = 1 << stage
+        return pltpu.make_async_remote_copy(
+            src_ref=held.at[pl.ds(0, size)],
+            dst_ref=held.at[pl.ds(size, size)],
+            send_sem=r.gather_send.at[kind - EMB, stage, group],
+            recv_sem=r.gather_recv.at[kind - EMB, stage, group],
+            device_id=place(flipped(me, gather_plans[group][stage]), experts_axis),
+            device_id_type=MESH,
+        )
+
+    def gather_begin(kind, rows):
+        for group, (first, wide) in enumerate(wide_groups):
+            r.held[kind - EMB][group][0] = rows[:, first : first + wide].astype(jnp.bfloat16)
+        for group in range(3):
+            gather_copy(kind, 0, group).start()
+
+    def gather_step(kind, stage):
+        for group in range(3):
+            gather_copy(kind, stage, group).wait()
+        if stage + 1 < bits:
+            for group in range(3):
+                gather_copy(kind, stage + 1, group).start()
+
+    def gathered(kind, group):
+        plan = gather_plans[group]
+        held = r.held[kind - EMB][group]
+        parts = []
+        for offset in range(n):
+            at = sum(1 << stage for stage in range(bits) if (offset >> plan[stage]) & 1)
+            parts.append(held[at].astype(jnp.float32))
+        return jnp.concatenate(parts, axis=0)
+
+    def unpacked(kind):
+        return r.into[kind][...].astype(jnp.float32).reshape(tokens, feature)
+
+    def trunk_rows(values, first, rows):
+        factor = lax.rsqrt(jnp.mean(values * values, axis=1, keepdims=True) + 1e-06)
+        normed = (values * factor * r.gain[...].reshape(1, feature)).astype(jnp.bfloat16)
+        hidden = values + jnp.dot(normed, r.tw[...], preferred_element_type=jnp.float32)
+        r.hidden[first : first + rows, :] = hidden.astype(jnp.bfloat16)
+        r.normed[:, first : first + rows] = dot_t(r.order[...], normed).astype(
+            jnp.bfloat16
+        )
+
+    def forward_rows(first, rows):
+        hidden = r.hidden[first : first + rows, :]
+        r.gate[first : first + rows, :] = jnp.dot(
+            hidden, r.wg[...], preferred_element_type=jnp.float32
+        )
+        r.up[first : first + rows, :] = jnp.dot(
+            hidden, r.wu[...], preferred_element_type=jnp.float32
+        )
+
+    def backward_rows(first, rows):
+        d_active = dot_t(r.cotan[first : first + rows, :], r.wd[...])
+        gate_pre = r.gate[first : first + rows, :]
+        up_pre = r.up[first : first + rows, :]
+        sigma = jax.nn.sigmoid(gate_pre)
+        silu_val = gate_pre * sigma
+        r.active[first : first + rows, :] = (silu_val * up_pre).astype(jnp.bfloat16)
+        r.d_gate[first : first + rows, :] = (
+            d_active * up_pre * sigma * (1.0 + gate_pre * (1.0 - sigma))
+        ).astype(jnp.bfloat16)
+        r.d_up[first : first + rows, :] = (d_active * silu_val).astype(jnp.bfloat16)
+
+    def rows_back(first, rows, column, wide):
+        r.d_rows[first : first + rows, column : column + wide] = (
+            dot_t(r.d_gate[first : first + rows, :], r.wg[column : column + wide, :])
+            + dot_t(r.d_up[first : first + rows, :], r.wu[column : column + wide, :])
+        ).astype(jnp.bfloat16)
+
+    for load in loads[5:]:
+        load.wait()
+    own[MARK].wait()
+    own[EMB].wait()
+    finish_kind(MARK)
+    finish_kind(EMB)
+
+    by_source = as_ones(
+        jnp.floor((iota((tokens, n), 0).astype(jnp.float32) + 0.5) / capacity).astype(jnp.int32)
+        == iota((tokens, n), 1)
+    )
+    marks_in = jnp.concatenate([r.into[MARK][device] for device in range(n)], axis=0)
+    spread = jnp.dot(by_source, marks_in.astype(jnp.bfloat16), preferred_element_type=jnp.float32)
+    lane = iota((tokens, LANES), 1)
+    within = iota((tokens, LANES), 0) & (capacity - 1)
+    flag = jnp.sum(jnp.where(lane == within, spread, 0.0), axis=1, keepdims=True)
+    before = as_ones(iota((tokens, tokens), 1) < iota((tokens, tokens), 0))
+    flag_wide = jnp.broadcast_to(flag, (tokens, LANES))
+    rank = jnp.dot(before, flag_wide.astype(jnp.bfloat16), preferred_element_type=jnp.float32)
+    chosen = jnp.where(rank.astype(jnp.int32) == lane, flag_wide, 0.0)
+    chooser = chosen.T[:hot_slots].astype(jnp.bfloat16)
+
+    got = unpacked(EMB)
+    gather_begin(EMB, jnp.dot(chooser, got.astype(jnp.bfloat16), preferred_element_type=jnp.float32))
+    start_batch(1)
+    trunk_rows(got, 0, tokens)
+    for stage in range(bits):
+        gather_step(EMB, stage)
+        if stage + 1 < bits:
+            start_batch(stage + 2)
+        if stage == 0:
+            forward_rows(0, tokens)
+
+    hot = jnp.concatenate([gathered(EMB, group) for group in range(3)], axis=1)
+    trunk_rows(hot, tokens, hot_rows)
+    forward_rows(tokens, hot_rows)
+
+    own[COT].wait()
+    finish_kind(COT)
+    got = unpacked(COT)
+    gather_begin(COT, jnp.dot(chooser, got.astype(jnp.bfloat16), preferred_element_type=jnp.float32))
+    r.cotan[0:tokens, :] = jnp.where(flag > 0, 0.0, got).astype(jnp.bfloat16)
+    backward_rows(0, tokens)
+    gather_step(COT, 0)
+    rows_back(0, tokens, 0, feature)
+    for stage in range(1, bits):
+        gather_step(COT, stage)
+    is_owner = popular == me
+    for group, (column, wide) in enumerate(wide_groups):
+        r.cotan[tokens : tokens + hot_rows, column : column + wide] = jnp.where(
+            is_owner, gathered(COT, group), 0.0
+        ).astype(jnp.bfloat16)
+    backward_rows(tokens, hot_rows)
+
+    def reduce_copy(stage, group):
+        bit = orders[group % 2][stage]
+        return pltpu.make_async_remote_copy(
+            src_ref=r.sent[stage][group],
+            dst_ref=r.came[stage][group],
+            send_sem=r.reduce_send.at[stage, group],
+            recv_sem=r.reduce_recv.at[stage, group],
+            device_id=place(flipped(me, bit), experts_axis),
+            device_id_type=MESH,
+        )
+
+    def pieces(stage, group, side):
+        size = feature >> (stage + 1)
+        bit = orders[group % 2][stage]
+        if stage == 1 and bit != layout[1]:
+            step = size // 2
+            return [(pl.multiple_of(part * size + side * step, 16), part * step, step) for part in range(2)]
+        return [(pl.multiple_of(side * size, size & -size), 0, size)]
+
+    def reduce_step(stage, group):
+        side = bit_of(me, orders[group % 2][stage])
+        kept, came = r.kept[stage - 1][group], r.came[stage - 1][group]
+        size = feature >> (stage + 1)
+        reduce_copy(stage - 1, group).wait()
+        if size % TILE:
+            total = kept[0 : 2 * size] + came[0 : 2 * size].astype(jnp.float32)
+            first, second = total[:size], total[size:]
+            r.sent[stage][group][0:size] = jnp.where(side == 1, first, second).astype(
+                jnp.bfloat16
+            )
+            reduce_copy(stage, group).start()
+            r.kept[stage][group][0:size] = jnp.where(side == 1, second, first)
+            return
+        for at, into, rows in pieces(stage, group, 1 - side):
+            r.sent[stage][group][into : into + rows] = (
+                kept[pl.ds(at, rows)] + came[pl.ds(at, rows)].astype(jnp.float32)
+            ).astype(jnp.bfloat16)
+        reduce_copy(stage, group).start()
+        for at, into, rows in pieces(stage, group, side):
+            r.kept[stage][group][into : into + rows] = kept[pl.ds(at, rows)] + came[
+                pl.ds(at, rows)
+            ].astype(jnp.float32)
+
+    side = bit_of(me, core)
+    half = feature // 2
+
+    def product(group, which):
+        column, wide = reduce_groups[group]
+        return jnp.dot(
+            r.normed[pl.ds(pl.multiple_of(which * half, half & -half), half), :],
+            r.d_rows[:, column : column + wide],
+            preferred_element_type=jnp.float32,
+        )
+
+    groups = range(len(reduce_groups))
+    rows_back(tokens, hot_rows, 0, feature)
+    for group in groups:
+        r.sent[0][group][...] = product(group, 1 - side).astype(jnp.bfloat16)
+        reduce_copy(0, group).start()
+        r.kept[0][group][...] = product(group, side)
+
+    work = []
+    for into, left, right in (
+        (r.grad_gate, r.hidden, r.d_gate),
+        (r.grad_up, r.hidden, r.d_up),
+        (r.grad_down, r.active, r.cotan),
+    ):
+        lines = into.shape[1]
+        for at, wide in reduce_widths(lines):
+
+            def one(into=into, left=left, right=right, at=at, wide=wide):
+                into[0, at : at + wide, :] = t_dot(
+                    left[:, at : at + wide], right[...]
+                ).astype(jnp.bfloat16)
+
+            work.append(one)
+    slots = (bits - 1) * len(reduce_groups)
+    done = 0
+    for stage in range(1, bits):
+        for group in groups:
+            reduce_step(stage, group)
+            slot_index = (stage - 1) * len(reduce_groups) + group + 1
+            while done < len(work) * slot_index // slots:
+                work[done]()
+                done += 1
+    for group in groups:
+        column, wide = reduce_groups[group]
+        reduce_copy(bits - 1, group).wait()
+        r.grad_trunk[:, column : column + wide] = r.kept[bits - 1][group][
+            0:share
+        ] + r.came[bits - 1][group][0:share].astype(jnp.float32)
+
+
+def fused_plan(n, hot_slots, tokens, feature, units):
+    bits = n.bit_length() - 1
+    rows = tokens + n * hot_slots
+    capacity = tokens // n
+    groups = reduce_widths(feature)
+    bf, f32 = jnp.bfloat16, jnp.float32
+    message = pltpu.VMEM((n, capacity, feature), bf)
+    mark = pltpu.VMEM((n, 1, LANES), f32)
+
+    def stages(kind):
+        sizes = [feature >> (stage + 1) for stage in range(bits)]
+        return [
+            [pltpu.VMEM((padded(size, TILE // 2), wide), kind) for _, wide in groups]
+            for size in sizes
+        ]
+
+    return dict(
+        tags=pltpu.VMEM((1, tokens), jnp.int32),
+        plan=pltpu.VMEM((1, n), jnp.int32),
+        helper=pltpu.VMEM((1, tokens), jnp.int32),
+        gain=pltpu.VMEM((feature,), f32),
+        emb=pltpu.VMEM((tokens, feature), bf),
+        cot=pltpu.VMEM((tokens, feature), bf),
+        tw=pltpu.VMEM((feature, feature), bf),
+        wg=pltpu.VMEM((feature, units), bf),
+        wu=pltpu.VMEM((feature, units), bf),
+        wd=pltpu.VMEM((units, feature), bf),
+        out=[mark, message, message],
+        into=[mark, message, message],
+        order=pltpu.VMEM((feature, feature), bf),
+        hidden=pltpu.VMEM((rows, feature), bf),
+        normed=pltpu.VMEM((feature, rows), bf),
+        cotan=pltpu.VMEM((rows, feature), bf),
+        gate=pltpu.VMEM((rows, units), f32),
+        up=pltpu.VMEM((rows, units), f32),
+        active=pltpu.VMEM((rows, units), bf),
+        d_gate=pltpu.VMEM((rows, units), bf),
+        d_up=pltpu.VMEM((rows, units), bf),
+        d_rows=pltpu.VMEM((rows, feature), bf),
+        held=[
+            [pltpu.VMEM((n, hot_slots, wide), bf) for _, wide in column_groups(feature)]
+            for _ in (EMB, COT)
+        ],
+        kept=stages(f32),
+        sent=stages(bf),
+        came=stages(bf),
+        load_sem=pltpu.SemaphoreType.DMA((10,)),
+        own_sem=pltpu.SemaphoreType.DMA((3,)),
+        send_sem=pltpu.SemaphoreType.DMA((3, n)),
+        recv_sem=pltpu.SemaphoreType.DMA((3, n)),
+        gather_send=pltpu.SemaphoreType.DMA((2, bits, 3)),
+        gather_recv=pltpu.SemaphoreType.DMA((2, bits, 3)),
+        reduce_send=pltpu.SemaphoreType.DMA((bits, len(groups))),
+        reduce_recv=pltpu.SemaphoreType.DMA((bits, len(groups))),
+    )
+
+
+def plan_bytes(plan):
+    total = 0
+    for item in jax.tree.leaves(plan):
+        if len(item.shape) > 1 and item.shape[-1] % LANES == 0:
+            lead = 1
+            for size in item.shape[:-2]:
+                lead *= size
+            lines = padded(item.shape[-2], TILE // 2)
+            total += lead * lines * item.shape[-1] * jnp.dtype(item.dtype).itemsize
+    return total
+
+
+def settle_kernel(count, *refs):
+    sems = refs[-1]
+    copies = [
+        pltpu.make_async_copy(refs[at], refs[count + at], sems.at[at]) for at in range(count)
+    ]
+    for copy in copies:
+        copy.start()
+    for copy in copies:
+        copy.wait()
+
+
+def settle(arrays):
+    return pl.pallas_call(
+        functools.partial(settle_kernel, len(arrays)),
+        out_shape=tuple(jax.ShapeDtypeStruct(array.shape, array.dtype) for array in arrays),
+        in_specs=[pl.BlockSpec(memory_space=pl.ANY)] * len(arrays),
+        out_specs=(pl.BlockSpec(memory_space=pltpu.HBM),) * len(arrays),
+        scratch_shapes=[pltpu.SemaphoreType.DMA((len(arrays),))],
+        compiler_params=pltpu.CompilerParams(vmem_limit_bytes=1024 * 1024),
+    )(*arrays)
+
+
+def fused_body(embeds, trunk_gain, trunk_weight, w_gate, w_up, w_down, tags, plan, helper, cotangent):
+    n = lax.axis_size(("dp", "expert"))
+    experts_axis = lax.axis_size("expert")
+    tokens, feature = embeds.shape
+    units = w_gate.shape[2]
+    hot_slots = tokens // 32
+    anywhere = pl.BlockSpec(memory_space=pltpu.HBM)
+    inside = pl.BlockSpec(memory_space=pltpu.VMEM)
+    inputs = dict(
+        emb_hbm=(embeds, anywhere),
+        gain_hbm=(trunk_gain, anywhere),
+        tw_hbm=(trunk_weight, anywhere),
+        wg_hbm=(w_gate, anywhere),
+        wu_hbm=(w_up, anywhere),
+        wd_hbm=(w_down, anywhere),
+        tags_hbm=(tags.reshape(1, tokens), anywhere),
+        plan_hbm=(plan.reshape(1, -1), anywhere),
+        helper_hbm=(helper.reshape(1, tokens), anywhere),
+        cot_hbm=(cotangent, anywhere),
+    )
+    outputs = dict(
+        grad_gate=jax.ShapeDtypeStruct(w_gate.shape, jnp.bfloat16),
+        grad_up=jax.ShapeDtypeStruct(w_up.shape, jnp.bfloat16),
+        grad_down=jax.ShapeDtypeStruct(w_down.shape, jnp.bfloat16),
+        grad_trunk=jax.ShapeDtypeStruct((feature // n, feature), jnp.float32),
+    )
+    scratch = fused_plan(n, hot_slots, tokens, feature, units)
+    names = (list(inputs) + list(outputs), jax.tree.structure(scratch))
+    results = pl.pallas_call(
+        functools.partial(fused_kernel, n, experts_axis, hot_slots, names),
+        out_shape=tuple(outputs.values()),
+        in_specs=[spec for _, spec in inputs.values()],
+        out_specs=(inside,) * len(outputs),
+        scratch_shapes=jax.tree.leaves(scratch),
+        compiler_params=pltpu.CompilerParams(
+            collective_id=0, has_side_effects=True, vmem_limit_bytes=VMEM_BYTES
+        ),
+    )(*[pltpu.with_memory_space_constraint(value, pltpu.HBM) for value, _ in inputs.values()])
+    return settle(results)
+
+
+def fits(embeds, w_gate, n):
+    tokens, feature = embeds.shape
+    units = w_gate.shape[2]
+    hot_slots = tokens // 32
+    if (tokens // n) % 8 or hot_slots % 8 or feature % (16 * n // 4):
+        return False
+    return plan_bytes(fused_plan(n, hot_slots, tokens, feature, units)) < VMEM_BYTES - 2 * 1024 * 1024
+
+
+def either(*args):
+    n = lax.axis_size(("dp", "expert"))
+    return (fused_body if fits(args[0], args[3], n) else body)(*args)
+
+
 def solution(mesh):
     spread_rows = P(("dp", "expert"), None)
     spread_first = P(("dp", "expert"), None, None)
     return jax.shard_map(
-        body,
+        either,
         mesh=mesh,
         in_specs=(
             spread_rows,

time: 122 us -> 90.8 us (0.74)
  matrix products: 26.9 us -> 0 us
  other arithmetic: 3.69 us -> 0 us
  Pallas kernels: 88.3 us -> 89.9 us
    dot_general x17 -> x0, matrix products: 26.9 us -> none  [the longest x3 8.91 us: t_dot(): lax.dot_general(a, b, (((0,), (0,)), ((), ())), preferred_element_type=jn...]
    pallas_call x3 -> x2, Pallas kernels: 88.3 us -> 89.9 us  [the longest x1 86.9 us: fused_body(): pl.pallas_call(functools.partial(fused_kernel, n, experts_axis, hot_slots...]
    reduce_sum x3 -> x0, other arithmetic: 1.35 us -> none  [the longest x1 0.93 us: body(): slot = jnp.sum(before.astype(jnp.int32), axis=1)]
    convert_element_type x1 -> x0, other arithmetic: 1.35 us -> none  [body(): ((tags == hot_expert) & (helper != hot_expert)).astype(jnp.bfloat16)]
where the time goes in v1:
time: 90.8 us; the launch traced here: 90.7 us
  Pallas kernels  89.9 us (99%)
    pallas_call x1, Pallas kernels, fused_body(): pl.pallas_call(functools.partial(fused_kernel, n, experts_axis, hot_slots...  86.9 us
    pallas_call x1, Pallas kernels, settle(): pl.pallas_call(functools.partial(settle_kernel, len(arrays)), out_shape=t...  3 us

profile of v1, /device:TPU:0, one launch (start us, length us, event | category | flops | bytes accessed | tf_op | source)
XLA Modules:
  0.0 90.7 jit_solution(2031943990538710345)
XLA Ops:
  0.6 86.9 %shard_map.129 = (bf16[1,1152,1024]{2,1,0:T(8,128)(2,1)S(1)}, bf16[1,1152,1024]{2,1,0:T(8,128)(2,1)S(1)}, bf16[1,1024,1152]{2,1,0:T(8,128)(2,1)S(1)}, f32[36,1152]{1,0:T(8,128)S(1)}) custom-call(bf16[256,1152]{1,0:T(8,128)(2,1)} %refs_0_.1, f32[1152]{0:T(1024)} %refs_1_.1, bf16[1152,1152]{1,0:T(8,128)(2,1)} %refs_2_.1, bf16[1,1152,1024]{2,1,0:T(8,128)(2,1)} %refs_3_.1, ...), custom_call_target="tpu_custom_call" | custom-call | tf_op jit(solution)/shard_map/pallas_call | solution.py:913
  87.5 3.0 %shard_map.130 = (bf16[1,1152,1024]{2,1,0:T(8,128)(2,1)}, bf16[1,1152,1024]{2,1,0:T(8,128)(2,1)}, bf16[1,1024,1152]{2,1,0:T(8,128)(2,1)}, f32[36,1152]{1,0:T(8,128)}) custom-call(bf16[1,1152,1024]{2,1,0:T(8,128)(2,1)S(1)} %get-tuple-element.8.refs_0_, bf16[1,1152,1024]{2,1,0:T(8,128)(2,1)S(1)} %get-tuple-element.9.refs_1_, ...), custom_call_target="tpu_custom_call" | custom-call | tf_op jit(solution)/shard_map/pallas_call | solution.py:875

commit v2 on v1

--- a/solution.py
+++ b/solution.py
@@ -12,6 +12,7 @@
 TILE = 16
 MESH = pl.DeviceIdType.MESH
 MARK, EMB, COT = range(3)
+WAVE = 99
 VMEM_BYTES = 45 * 1024 * 1024
 
 
@@ -441,6 +442,11 @@
     return list(zip(starts, widths))
 
 
+def gather_orders(n, experts_axis):
+    core, flat, tall, *middle = reduce_orders(n, experts_axis)[0]
+    return {EMB: [[middle, [flat], [tall], [core]], [middle, [tall], [flat], [core]], [middle, [flat], [tall], [core]]], COT: [[middle, [flat, tall], [core]], [[flat, tall], middle, [core]], [middle, [flat, tall], [core]]]}
+
+
 def fused_kernel(n, experts_axis, hot_slots, names, *refs):
     plain, tree = names
     r = types.SimpleNamespace(
@@ -453,9 +459,9 @@
     hot_rows = n * hot_slots
     share = feature // n
     me = flat_index(experts_axis)
-    wide_groups = column_groups(feature)
-    core, gather_orders = axis_orders(n, experts_axis)
-    gather_plans = [order[::-1] + [core] for order in gather_orders]
+    core = experts_axis.bit_length() - 1
+    gather_groups = column_groups(feature)
+    gather_plans = gather_orders(n, experts_axis)
     reduce_groups = reduce_widths(feature)
     orders = reduce_orders(n, experts_axis)
     layout = orders[0]
@@ -537,7 +543,8 @@
         lax.fori_loop(first, last, start, 0)
 
     def start_batch(batch):
-        cuts = [1 + (n - 1) * at // (bits + 1) for at in range(bits + 2)]
+        parts = len(gather_plans[EMB][0]) + 1
+        cuts = [1 + (n - 1) * at // parts for at in range(parts + 1)]
         start_kinds(cuts[batch], cuts[batch + 1], COT)
 
     def finish_kind(kind):
@@ -571,37 +578,48 @@
         source = source + part * (share << bit)
     r.order[...] = as_ones(source == iota((feature, feature), 1))
 
-    def gather_copy(kind, stage, group):
-        held = r.held[kind - EMB][group]
-        size = 1 << stage
-        return pltpu.make_async_remote_copy(
-            src_ref=held.at[pl.ds(0, size)],
-            dst_ref=held.at[pl.ds(size, size)],
-            send_sem=r.gather_send.at[kind - EMB, stage, group],
-            recv_sem=r.gather_recv.at[kind - EMB, stage, group],
-            device_id=place(flipped(me, gather_plans[group][stage]), experts_axis),
-            device_id_type=MESH,
-        )
+    def gather_copies(kind, stage):
+        copies = []
+        for group in range(len(gather_groups)):
+            steps = gather_plans[kind][group]
+            held = r.held[kind - EMB][group]
+            size = 1 << sum(len(step) for step in steps[:stage])
+            for mask in range(1, 1 << len(steps[stage])):
+                other = me
+                for position, bit in enumerate(steps[stage]):
+                    if (mask >> position) & 1:
+                        other = flipped(other, bit)
+                copies.append(
+                    pltpu.make_async_remote_copy(
+                        src_ref=held.at[pl.ds(0, size)],
+                        dst_ref=held.at[pl.ds(mask * size, size)],
+                        send_sem=r.gather_send.at[kind - EMB, stage, group, mask],
+                        recv_sem=r.gather_recv.at[kind - EMB, stage, group, mask],
+                        device_id=place(other, experts_axis),
+                        device_id_type=MESH,
+                    )
+                )
+        return copies
 
     def gather_begin(kind, rows):
-        for group, (first, wide) in enumerate(wide_groups):
+        for group, (first, wide) in enumerate(gather_groups):
             r.held[kind - EMB][group][0] = rows[:, first : first + wide].astype(jnp.bfloat16)
-        for group in range(3):
-            gather_copy(kind, 0, group).start()
+        for copy in gather_copies(kind, 0):
+            copy.start()
 
     def gather_step(kind, stage):
-        for group in range(3):
-            gather_copy(kind, stage, group).wait()
-        if stage + 1 < bits:
-            for group in range(3):
-                gather_copy(kind, stage + 1, group).start()
+        for copy in gather_copies(kind, stage):
+            copy.wait()
+        if stage + 1 < len(gather_plans[kind][0]):
+            for copy in gather_copies(kind, stage + 1):
+                copy.start()
 
     def gathered(kind, group):
-        plan = gather_plans[group]
+        plan = sum(gather_plans[kind][group], [])
         held = r.held[kind - EMB][group]
         parts = []
         for offset in range(n):
-            at = sum(1 << stage for stage in range(bits) if (offset >> plan[stage]) & 1)
+            at = sum(1 << position for position in range(bits) if (offset >> plan[position]) & 1)
             parts.append(held[at].astype(jnp.float32))
         return jnp.concatenate(parts, axis=0)
 
@@ -643,6 +661,21 @@
             dot_t(r.d_gate[first : first + rows, :], r.wg[column : column + wide, :])
             + dot_t(r.d_up[first : first + rows, :], r.wu[column : column + wide, :])
         ).astype(jnp.bfloat16)
+
+    side = bit_of(me, core)
+    half = feature // 2
+
+    def product(group, which, first, rows):
+        column, wide = reduce_groups[group]
+        return jnp.dot(
+            r.normed[
+                pl.ds(pl.multiple_of(which * half, half & -half), half), first : first + rows
+            ],
+            r.d_rows[first : first + rows, column : column + wide],
+            preferred_element_type=jnp.float32,
+        )
+
+    groups = range(len(reduce_groups))
 
     for load in loads[5:]:
         load.wait()
@@ -670,14 +703,14 @@
     gather_begin(EMB, jnp.dot(chooser, got.astype(jnp.bfloat16), preferred_element_type=jnp.float32))
     start_batch(1)
     trunk_rows(got, 0, tokens)
-    for stage in range(bits):
+    for stage in range(len(gather_plans[EMB][0])):
         gather_step(EMB, stage)
-        if stage + 1 < bits:
+        if stage + 1 < len(gather_plans[EMB][0]):
             start_batch(stage + 2)
         if stage == 0:
             forward_rows(0, tokens)
 
-    hot = jnp.concatenate([gathered(EMB, group) for group in range(3)], axis=1)
+    hot = jnp.concatenate([gathered(EMB, group) for group in range(len(gather_groups))], axis=1)
     trunk_rows(hot, tokens, hot_rows)
     forward_rows(tokens, hot_rows)
 
@@ -689,10 +722,15 @@
     backward_rows(0, tokens)
     gather_step(COT, 0)
     rows_back(0, tokens, 0, feature)
-    for stage in range(1, bits):
+    for group in groups:
+        r.ahead[group][...] = product(group, 1 - side, 0, tokens)
+    gather_step(COT, 1)
+    for group in groups:
+        r.kept[0][group][...] = product(group, side, 0, tokens)
+    for stage in range(2, len(gather_plans[COT][0])):
         gather_step(COT, stage)
     is_owner = popular == me
-    for group, (column, wide) in enumerate(wide_groups):
+    for group, (column, wide) in enumerate(gather_groups):
         r.cotan[tokens : tokens + hot_rows, column : column + wide] = jnp.where(
             is_owner, gathered(COT, group), 0.0
         ).astype(jnp.bfloat16)
@@ -741,24 +779,6 @@
                 pl.ds(at, rows)
             ].astype(jnp.float32)
 
-    side = bit_of(me, core)
-    half = feature // 2
-
-    def product(group, which):
-        column, wide = reduce_groups[group]
-        return jnp.dot(
-            r.normed[pl.ds(pl.multiple_of(which * half, half & -half), half), :],
-            r.d_rows[:, column : column + wide],
-            preferred_element_type=jnp.float32,
-        )
-
-    groups = range(len(reduce_groups))
-    rows_back(tokens, hot_rows, 0, feature)
-    for group in groups:
-        r.sent[0][group][...] = product(group, 1 - side).astype(jnp.bfloat16)
-        reduce_copy(0, group).start()
-        r.kept[0][group][...] = product(group, side)
-
     work = []
     for into, left, right in (
         (r.grad_gate, r.hidden, r.d_gate),
@@ -774,15 +794,29 @@
                 ).astype(jnp.bfloat16)
 
             work.append(one)
-    slots = (bits - 1) * len(reduce_groups)
+    rows_back(tokens, hot_rows, 0, feature)
+
+    def first_step(group):
+        r.sent[0][group][...] = (
+            r.ahead[group][...] + product(group, 1 - side, tokens, hot_rows)
+        ).astype(jnp.bfloat16)
+        reduce_copy(0, group).start()
+        r.kept[0][group][...] += product(group, side, tokens, hot_rows)
+
+    steps = sorted(
+        ((stage, group) for stage in range(bits) for group in groups),
+        key=lambda step: (step[1] + WAVE * step[0], -step[0]),
+    )
     done = 0
-    for stage in range(1, bits):
-        for group in groups:
+    later = len(reduce_groups) + 1
+    for index, (stage, group) in enumerate(steps):
+        if stage == 0:
+            first_step(group)
+        else:
             reduce_step(stage, group)
-            slot_index = (stage - 1) * len(reduce_groups) + group + 1
-            while done < len(work) * slot_index // slots:
-                work[done]()
-                done += 1
+        while done * (len(steps) - later) < len(work) * (index + 1 - later):
+            work[done]()
+            done += 1
     for group in groups:
         column, wide = reduce_groups[group]
         reduce_copy(bits - 1, group).wait()
@@ -835,14 +869,15 @@
             for _ in (EMB, COT)
         ],
         kept=stages(f32),
+        ahead=stages(f32)[0],
         sent=stages(bf),
         came=stages(bf),
         load_sem=pltpu.SemaphoreType.DMA((10,)),
         own_sem=pltpu.SemaphoreType.DMA((3,)),
         send_sem=pltpu.SemaphoreType.DMA((3, n)),
         recv_sem=pltpu.SemaphoreType.DMA((3, n)),
-        gather_send=pltpu.SemaphoreType.DMA((2, bits, 3)),
-        gather_recv=pltpu.SemaphoreType.DMA((2, bits, 3)),
+        gather_send=pltpu.SemaphoreType.DMA((2, bits, 3, 4)),
+        gather_recv=pltpu.SemaphoreType.DMA((2, bits, 3, 4)),
         reduce_send=pltpu.SemaphoreType.DMA((bits, len(groups))),
         reduce_recv=pltpu.SemaphoreType.DMA((bits, len(groups))),
     )

time: 90.8 us -> 86.4 us (0.952)
  Pallas kernels: 89.9 us -> 85.4 us
    pallas_call x1, Pallas kernels: 86.9 us -> 82.4 us  [fused_body(): pl.pallas_call(functools.partial(fused_kernel, n, experts_axis, hot_slots...]
where the time goes in v2:
time: 86.4 us; the launch traced here: 86.2 us
  Pallas kernels  85.4 us (99%)
    pallas_call x1, Pallas kernels, fused_body(): pl.pallas_call(functools.partial(fused_kernel, n, experts_axis, hot_slots...  82.4 us
    pallas_call x1, Pallas kernels, settle(): pl.pallas_call(functools.partial(settle_kernel, len(arrays)), out_shape=t...  3 us

profile of v2, /device:TPU:0, one launch (start us, length us, event | category | flops | bytes accessed | tf_op | source)
XLA Modules:
  0.0 86.2 jit_solution(12169019687372851381)
XLA Ops:
  0.6 82.4 %shard_map.129 = (bf16[1,1152,1024]{2,1,0:T(8,128)(2,1)S(1)}, bf16[1,1152,1024]{2,1,0:T(8,128)(2,1)S(1)}, bf16[1,1024,1152]{2,1,0:T(8,128)(2,1)S(1)}, f32[36,1152]{1,0:T(8,128)S(1)}) custom-call(bf16[256,1152]{1,0:T(8,128)(2,1)} %refs_0_.1, f32[1152]{0:T(1024)} %refs_1_.1, bf16[1152,1152]{1,0:T(8,128)(2,1)} %refs_2_.1, bf16[1,1152,1024]{2,1,0:T(8,128)(2,1)} %refs_3_.1, ...), custom_call_target="tpu_custom_call" | custom-call | tf_op jit(solution)/shard_map/pallas_call | solution.py:948
  83.0 3.0 %shard_map.130 = (bf16[1,1152,1024]{2,1,0:T(8,128)(2,1)}, bf16[1,1152,1024]{2,1,0:T(8,128)(2,1)}, bf16[1,1024,1152]{2,1,0:T(8,128)(2,1)}, f32[36,1152]{1,0:T(8,128)}) custom-call(bf16[1,1152,1024]{2,1,0:T(8,128)(2,1)S(1)} %get-tuple-element.8.refs_0_, bf16[1,1152,1024]{2,1,0:T(8,128)(2,1)S(1)} %get-tuple-element.9.refs_1_, ...), custom_call_target="tpu_custom_call" | custom-call | tf_op jit(solution)/shard_map/pallas_call | solution.py:910

commit v3 on v2

--- a/solution.py
+++ b/solution.py
@@ -465,6 +465,7 @@
     reduce_groups = reduce_widths(feature)
     orders = reduce_orders(n, experts_axis)
     layout = orders[0]
+    lasts = 1 << (bits - 3)
 
     barrier = pltpu.get_barrier_semaphore()
 
@@ -755,20 +756,45 @@
             return [(pl.multiple_of(part * size + side * step, 16), part * step, step) for part in range(2)]
         return [(pl.multiple_of(side * size, size & -size), 0, size)]
 
+    def last_copies(group):
+        copies = []
+        for mask in range(1, lasts):
+            other = me
+            for position, bit in enumerate(layout[:2:-1]):
+                if (mask >> position) & 1:
+                    other = flipped(other, bit)
+            copies.append(
+                pltpu.make_async_remote_copy(
+                    src_ref=r.last_out[group].at[mask],
+                    dst_ref=r.last_in[group].at[mask],
+                    send_sem=r.last_send.at[group, mask],
+                    recv_sem=r.last_recv.at[group, mask],
+                    device_id=place(other, experts_axis),
+                    device_id_type=MESH,
+                )
+            )
+        return copies
+
+    def last_step(group):
+        reduce_copy(2, group).wait()
+        total = r.kept[2][group][...] + r.came[2][group][...].astype(jnp.float32)
+        blocks = [total[at * share : (at + 1) * share] for at in range(lasts)]
+        for position, bit in enumerate(layout[:2:-1]):
+            swap = bit_of(me, bit) == 1
+            blocks = [
+                jnp.where(swap, blocks[at ^ (1 << position)], blocks[at]) for at in range(lasts)
+            ]
+        for mask in range(1, lasts):
+            r.last_out[group][mask, 0:share] = blocks[mask].astype(jnp.bfloat16)
+        for copy in last_copies(group):
+            copy.start()
+        r.last_kept[group][0:share] = blocks[0]
+
     def reduce_step(stage, group):
         side = bit_of(me, orders[group % 2][stage])
         kept, came = r.kept[stage - 1][group], r.came[stage - 1][group]
         size = feature >> (stage + 1)
         reduce_copy(stage - 1, group).wait()
-        if size % TILE:
-            total = kept[0 : 2 * size] + came[0 : 2 * size].astype(jnp.float32)
-            first, second = total[:size], total[size:]
-            r.sent[stage][group][0:size] = jnp.where(side == 1, first, second).astype(
-                jnp.bfloat16
-            )
-            reduce_copy(stage, group).start()
-            r.kept[stage][group][0:size] = jnp.where(side == 1, second, first)
-            return
         for at, into, rows in pieces(stage, group, 1 - side):
             r.sent[stage][group][into : into + rows] = (
                 kept[pl.ds(at, rows)] + came[pl.ds(at, rows)].astype(jnp.float32)
@@ -804,7 +830,7 @@
         r.kept[0][group][...] += product(group, side, tokens, hot_rows)
 
     steps = sorted(
-        ((stage, group) for stage in range(bits) for group in groups),
+        ((stage, group) for stage in range(4) for group in groups),
         key=lambda step: (step[1] + WAVE * step[0], -step[0]),
     )
     done = 0
@@ -812,6 +838,8 @@
     for index, (stage, group) in enumerate(steps):
         if stage == 0:
             first_step(group)
+        elif stage == 3:
+            last_step(group)
         else:
             reduce_step(stage, group)
         while done * (len(steps) - later) < len(work) * (index + 1 - later):
@@ -819,10 +847,12 @@
             done += 1
     for group in groups:
         column, wide = reduce_groups[group]
-        reduce_copy(bits - 1, group).wait()
-        r.grad_trunk[:, column : column + wide] = r.kept[bits - 1][group][
-            0:share
-        ] + r.came[bits - 1][group][0:share].astype(jnp.float32)
+        for copy in last_copies(group):
+            copy.wait()
+        total = r.last_kept[group][0:share]
+        for mask in range(1, lasts):
+            total = total + r.last_in[group][mask, 0:share].astype(jnp.float32)
+        r.grad_trunk[:, column : column + wide] = total
 
 
 def fused_plan(n, hot_slots, tokens, feature, units):
@@ -831,11 +861,12 @@
     capacity = tokens // n
     groups = reduce_widths(feature)
     bf, f32 = jnp.bfloat16, jnp.float32
+    block = padded(feature // n, TILE // 2)
     message = pltpu.VMEM((n, capacity, feature), bf)
     mark = pltpu.VMEM((n, 1, LANES), f32)
 
     def stages(kind):
-        sizes = [feature >> (stage + 1) for stage in range(bits)]
+        sizes = [feature >> (stage + 1) for stage in range(3)]
         return [
             [pltpu.VMEM((padded(size, TILE // 2), wide), kind) for _, wide in groups]
             for size in sizes
@@ -870,6 +901,11 @@
         ],
         kept=stages(f32),
         ahead=stages(f32)[0],
+        last_kept=[pltpu.VMEM((block, wide), f32) for _, wide in groups],
+        last_out=[pltpu.VMEM((1 << (bits - 3), block, wide), bf) for _, wide in groups],
+        last_in=[pltpu.VMEM((1 << (bits - 3), block, wide), bf) for _, wide in groups],
+        last_send=pltpu.SemaphoreType.DMA((len(groups), 1 << (bits - 3))),
+        last_recv=pltpu.SemaphoreType.DMA((len(groups), 1 << (bits - 3))),
         sent=stages(bf),
         came=stages(bf),
         load_sem=pltpu.SemaphoreType.DMA((10,)),
@@ -878,8 +914,8 @@
         recv_sem=pltpu.SemaphoreType.DMA((3, n)),
         gather_send=pltpu.SemaphoreType.DMA((2, bits, 3, 4)),
         gather_recv=pltpu.SemaphoreType.DMA((2, bits, 3, 4)),
-        reduce_send=pltpu.SemaphoreType.DMA((bits, len(groups))),
-        reduce_recv=pltpu.SemaphoreType.DMA((bits, len(groups))),
+        reduce_send=pltpu.SemaphoreType.DMA((3, len(groups))),
+        reduce_recv=pltpu.SemaphoreType.DMA((3, len(groups))),
     )
 
 
@@ -962,7 +998,7 @@
     tokens, feature = embeds.shape
     units = w_gate.shape[2]
     hot_slots = tokens // 32
-    if (tokens // n) % 8 or hot_slots % 8 or feature % (16 * n // 4):
+    if n < 16 or (tokens // n) % 8 or hot_slots % 8 or feature % (16 * n // 4):
         return False
     return plan_bytes(fused_plan(n, hot_slots, tokens, feature, units)) < VMEM_BYTES - 2 * 1024 * 1024
 

time: 86.4 us -> 86.6 us (level)
  no operation moved by 1% of the time
where the time goes in v3:
time: 86.6 us; the launch traced here: 86.4 us
  Pallas kernels  85.6 us (99%)
    pallas_call x1, Pallas kernels, fused_body(): pl.pallas_call(functools.partial(fused_kernel, n, experts_axis, hot_slots...  82.6 us
    pallas_call x1, Pallas kernels, settle(): pl.pallas_call(functools.partial(settle_kernel, len(arrays)), out_shape=t...  3 us

profile of v3, /device:TPU:0, one launch (start us, length us, event | category | flops | bytes accessed | tf_op | source)
XLA Modules:
  0.0 86.4 jit_solution(15805939651151501155)
XLA Ops:
  0.6 82.6 %shard_map.129 = (bf16[1,1152,1024]{2,1,0:T(8,128)(2,1)S(1)}, bf16[1,1152,1024]{2,1,0:T(8,128)(2,1)S(1)}, bf16[1,1024,1152]{2,1,0:T(8,128)(2,1)S(1)}, f32[36,1152]{1,0:T(8,128)S(1)}) custom-call(bf16[256,1152]{1,0:T(8,128)(2,1)} %refs_0_.1, f32[1152]{0:T(1024)} %refs_1_.1, bf16[1152,1152]{1,0:T(8,128)(2,1)} %refs_2_.1, bf16[1,1152,1024]{2,1,0:T(8,128)(2,1)} %refs_3_.1, ...), custom_call_target="tpu_custom_call" | custom-call | tf_op jit(solution)/shard_map/pallas_call | solution.py:984
  83.3 3.0 %shard_map.130 = (bf16[1,1152,1024]{2,1,0:T(8,128)(2,1)}, bf16[1,1152,1024]{2,1,0:T(8,128)(2,1)}, bf16[1,1024,1152]{2,1,0:T(8,128)(2,1)}, f32[36,1152]{1,0:T(8,128)}) custom-call(bf16[1,1152,1024]{2,1,0:T(8,128)(2,1)S(1)} %get-tuple-element.8.refs_0_, bf16[1,1152,1024]{2,1,0:T(8,128)(2,1)S(1)} %get-tuple-element.9.refs_1_, ...), custom_call_target="tpu_custom_call" | custom-call | tf_op jit(solution)/shard_map/pallas_call | solution.py:946
